TPU v7x, 256 devices: a whole 4x4x8 slice. The times are simulated.
256 devices in a mesh: seq: 64 (over y_hi, z, x), user: 4 (over y_lo, core).
Axes of the slice: x: 4, y: 4 (y_hi: 2, y_lo: 2; y = y_hi * 2 + y_lo), z: 8, core: 2. Of those that a mesh axis runs over, the one named last changes fastest.
Arguments:
- history: bfloat16 [4, 32768, 1024], P('user', 'seq'), may hold values from -6 to 6
- hist_len: int32 [4], P('user'), may hold values from 16384 to 32768, as said below
- cand_start: int32 [4, 16], P('user'), may hold values from 0 to 127
- candidates: bfloat16 [4, 2048, 1024], P('user', 'seq'), may hold values from -6 to 6
- slot_cand: int32 [4, 2048], P('user', 'seq'), may hold values from 0 to 2047, each once within a row
- w_kv: bfloat16 [1024, 2048], P('user'), may hold values from -0.1875 to 0.1875
- w_qu: bfloat16 [1024, 2048], P('user'), may hold values from -0.1875 to 0.1875
- w_o: bfloat16 [1024, 1024], P('user'), may hold values from -0.1875 to 0.1875
Outputs:
- scored: bfloat16 [4, 2048, 1024], P('user', 'seq')
Inputs may be any that keep to these rules, and one draw needn't show every extreme that they name: `hist_len`: some user has exactly 32768 positions and another exactly 16384. `slot_cand`: each user's slots hold each of its 2048 candidates once.
All inputs are finite; a program needn't handle non-finite values.
Results may differ from a plain program's by a relative error of at most 0.007.
Values may be sent and summed in bfloat16 or wider, within the bound.
A program may use at most 64 MiB of HBM per device.

v0:
```python
import jax
import jax.numpy as jnp
from jax import lax
from jax.sharding import PartitionSpec as P

H = 32
CB = 128
KBLK = 128


def layer_norm(rows):
    rows = rows.astype(jnp.float32)
    center = rows - jnp.mean(rows, axis=-1, keepdims=True)
    spread = jnp.mean(center * center, axis=-1, keepdims=True)
    return center / jnp.sqrt(spread + 1e-05)


def attend(queries, keys, values, visible):
    count = queries.shape[0]
    length = keys.shape[0]
    width = queries.shape[1]
    head_size = width // H
    group = min(8, H)
    groups = H // group
    q_heads = queries.reshape(count, groups, group, head_size).transpose(1, 0, 2, 3)
    k_heads = keys.reshape(length, groups, group, head_size).transpose(1, 0, 2, 3)
    v_heads = values.reshape(length, groups, group, head_size).transpose(1, 0, 2, 3)

    def one_group(items):
        q_part, k_part, v_part = items
        scores = jnp.einsum("rgd,kgd->grk", q_part, k_part, preferred_element_type=jnp.float32)
        weights = jnp.where(visible[None], jax.nn.silu(scores), 0.0).astype(jnp.bfloat16)
        return jnp.einsum("grk,kgd->rgd", weights, v_part, preferred_element_type=jnp.float32)

    result = lax.map(one_group, (q_heads, k_heads, v_heads))
    return result.transpose(1, 0, 2, 3).reshape(count, width)


def local(history, hist_len, cand_start, candidates, slot_cand, w_kv, w_qu, w_o):
    hist_rows = history[0]
    cand_rows = candidates[0]
    hist_count = hist_rows.shape[0]
    width = cand_rows.shape[1]
    normed_hist = layer_norm(hist_rows).astype(jnp.bfloat16)
    normed_cand = layer_norm(cand_rows).astype(jnp.bfloat16)
    key_value = jnp.dot(
        normed_hist,
        lax.all_gather(w_kv, "user", axis=0, tiled=True),
        preferred_element_type=jnp.float32,
    )
    query_gate = jnp.dot(
        normed_cand,
        lax.all_gather(w_qu, "user", axis=0, tiled=True),
        preferred_element_type=jnp.float32,
    )
    key_value = jax.nn.silu(key_value).astype(jnp.bfloat16)
    keys = key_value[:, :width]
    values = key_value[:, width:]
    query_gate = jax.nn.silu(query_gate)
    queries = query_gate[:, :width].astype(jnp.bfloat16)
    gates = query_gate[:, width:]
    all_queries, all_slots = (
        lax.all_gather(queries, "seq", axis=0, tiled=True),
        lax.all_gather(slot_cand[0], "seq", axis=0, tiled=True),
    )
    length = hist_len[0]
    starts = cand_start[0] * KBLK
    positions = lax.axis_index("seq") * hist_count + jnp.arange(hist_count, dtype=jnp.int32)

    def partial_rows(q_rows, lows):
        count = q_rows.shape[0]

        def compute():
            visible = (positions[None, :] >= lows[:, None]) & (positions[None, :] < length)
            return attend(q_rows, keys, values, visible)

        active = (jnp.min(lows) <= positions[-1]) & (positions[0] < length)
        return lax.cond(active, compute, lambda: jnp.zeros((count, width), jnp.float32))

    block_of = (all_slots // CB)[:, None] == jnp.arange(starts.shape[0], dtype=jnp.int32)[None, :]
    slot_lows = jnp.sum(jnp.where(block_of, starts[None, :], 0), axis=1)
    q_rows = all_queries
    lows = slot_lows
    count = q_rows.shape[0]
    q_blocks = q_rows.reshape(count // 512, 512, width)
    low_blocks = lows.reshape(count // 512, 512)
    result = lax.map(lambda items: partial_rows(items[0], items[1]), (q_blocks, low_blocks))
    summed = lax.psum_scatter(result.reshape(count, width), "seq", scatter_dimension=0, tiled=True)
    normed_mix = layer_norm(summed).astype(jnp.bfloat16)
    gated = (lax.optimization_barrier(normed_mix).astype(jnp.float32) * gates).astype(jnp.bfloat16)
    projected = jnp.dot(
        gated, lax.all_gather(w_o, "user", axis=0, tiled=True), preferred_element_type=jnp.float32
    )
    return (cand_rows.astype(jnp.float32) + projected).astype(jnp.bfloat16)[None]


def solution(mesh):
    in_specs = (
        P("user", "seq", None),
        P("user"),
        P("user", None),
        P("user", "seq", None),
        P("user", "seq"),
        P("user", None),
        P("user", None),
        P("user", None),
    )
    out_specs = P("user", "seq", None)
    return jax.shard_map(local, mesh=mesh, in_specs=in_specs, out_specs=out_specs, check_vma=False)
```

profile of v0, /device:TPU:8, one launch (start us, length us, event | category | flops | bytes accessed | tf_op | source)
XLA Modules:
  0.0 781.6 jit_solution(9543892753730595389)
XLA Ops:
  9.0 1.0 fusion.37
  10.1 49.4 %all-gather.6.cloned.1.call-done = bf16[1024,2048]{1,0:T(8,128)(2,1)} async-done(((bf16[256,2048]{1,0:T(8,128)(2,1)}), bf16[1024,2048]{1,0:T(8,128)(2,1)}) %all-gather.6.cloned.1.call-update) | async-done | bytes 4194320 | tf_op jit(solution)/shard_map/all_gather | solution.py:53
  59.5 3.1 divide_multiply_fusion
  65.5 25.5 %all-reduce = s32[2048]{0:T(1024)S(1)} all-reduce(s32[2048]{0:T(1024)S(1)} %bitcast_dynamic-update-slice_fusion), channel_id=2, replica_groups=mesh['seq'=64,'user'=4] {'seq'}, use_global_device_ids=true, to_apply=%add | all-reduce | flops 2048 | bytes 16384 | tf_op jit(solution)/shard_map/all_gather | solution.py:64
  93.5 18.0 %all-gather.10.cloned.1.call-done = bf16[1024,2048]{1,0:T(8,128)(2,1)} async-done(((bf16[256,2048]{1,0:T(8,128)(2,1)}), bf16[1024,2048]{1,0:T(8,128)(2,1)}) %all-gather.10.cloned.1.call-update) | async-done | bytes 4194320 | tf_op jit(solution)/shard_map/all_gather | solution.py:48
  111.5 5.1 multiply_convert_fusion
  117.4 1.3 copy.15
  118.7 126.1 %all-gather.8.cloned.1.call-done = bf16[2048,1024]{1,0:T(8,128)(2,1)} async-done(((bf16[32,1024]{1,0:T(8,128)(2,1)}), bf16[2048,1024]{1,0:T(8,128)(2,1)}) %all-gather.8.cloned.1.call-update) | async-done | bytes 4194320 | tf_op jit(solution)/shard_map/all_gather | solution.py:63
  244.8 6.2 copy.13
  251.0 30.2 %while.25 = (s32[]{:T(128)}, f32[4,512,1024]{2,1,0:T(8,128)}, s32[4,512]{1,0:T(4,128)S(1)}, s32[512]{0:T(512)S(1)}, pred[]{:T(512)}, /*index=5*/bf16[4,512,1024]...) while((s32[]{:T(128)}, f32[4,512,1024]{2,1,0:T(8,128)}, ...), condition=%wide.region_11.12_spmd, body=%wide.region_5.11_spmd.sunk | while | flops 281543680 | bytes 12334971 | solution.py:87
  253.5 1.6 conditional.2
  253.5 1.6 broadcast_in_dim.38
  255.2 1.9 copy.26
  257.1 1.5 constant_dynamic-update-slice_fusion.2
  261.1 1.6 conditional.2
  261.1 1.6 broadcast_in_dim.38
  262.7 1.9 copy.26
  264.7 1.4 constant_dynamic-update-slice_fusion.2
  268.6 1.6 conditional.2
  268.6 1.6 broadcast_in_dim.38
  270.3 1.9 copy.26
  272.2 1.5 constant_dynamic-update-slice_fusion.2
  276.2 1.6 conditional.2
  276.2 1.6 broadcast_in_dim.38
  277.8 1.9 copy.26
  279.7 1.5 constant_dynamic-update-slice_fusion.2
  281.8 466.2 %reduce-scatter.2.cloned.1.call-done = f32[32,1024]{1,0:T(8,128)} async-done(((f32[2048,1024]{1,0:T(8,128)}), f32[32,1024]{1,0:T(8,128)}) %reduce-scatter.2.cloned.1.call-update) | async-done | bytes 131088 | tf_op jit(solution)/shard_map/reduce_scatter | solution.py:88
  748.0 1.0 reduce_sum.68
  749.0 1.1 multiply_reduce_fusion
  750.2 1.0 divide_convert_fusion
  751.2 21.3 %all-gather.12.cloned.1.call-done = bf16[1024,1024]{1,0:T(8,128)(2,1)} async-done(((bf16[256,1024]{1,0:T(8,128)(2,1)}), bf16[1024,1024]{1,0:T(8,128)(2,1)}) %all-gather.12.cloned.1.call-update) | async-done | bytes 2097168 | tf_op jit(solution)/shard_map/all_gather | solution.py:92
  772.4 2.7 fusion.27
  (54 shorter events, 12.2 us)
Async XLA Ops:
  6.5 57.6 %copy-start.6 = (u32[256]{0:T(256)S(1)}, u32[256]{0:T(256)}, u32[]{:S(2)}) copy-start(u32[256]{0:T(256)} %constant.98) | copy-start | bytes 3076
  6.5 58.8 %copy-start.4 = (s32[1,32]{1,0:T(1,128)S(1)}, s32[1,32]{1,0:T(1,128)}, u32[]{:S(2)}) copy-start(s32[1,32]{1,0:T(1,128)} %param.18) | copy-start | bytes 388
  6.5 84.5 %copy-start.5 = (s32[1,16]{1,0:T(1,128)S(1)}, s32[1,16]{1,0:T(1,128)}, u32[]{:S(2)}) copy-start(s32[1,16]{1,0:T(1,128)} %param.16) | copy-start | bytes 196
  6.5 86.3 %copy-start = (bf16[1,512,1024]{2,1,0:T(8,128)(2,1)S(1)}, bf16[1,512,1024]{2,1,0:T(8,128)(2,1)}, u32[]{:S(2)}) copy-start(bf16[1,512,1024]{2,1,0:T(8,128)(2,1)} %param.14) | copy-start | bytes 3145732
  6.5 53.0 %all-gather.6.cloned.1.call-start = ((), (), s32[]{:S(2)}) async-start(), calls=%async_computation.1 | async-start | bytes 5242880 | tf_op jit(solution)/shard_map/all_gather | solution.py:53
  7.3 104.3 %all-gather.10.cloned.1.call-start = ((), (), s32[]{:S(2)}) async-start(), calls=%async_computation.3 | async-start | bytes 5242880 | tf_op jit(solution)/shard_map/all_gather | solution.py:48
  8.0 236.8 %all-gather.8.cloned.1.call-start = ((), (), s32[]{:S(2)}) async-start(), calls=%async_computation.2 | async-start | bytes 4259840 | tf_op jit(solution)/shard_map/all_gather | solution.py:63
  62.7 0.7 copy-start.2
  64.0 684.0 %reduce-scatter.2.cloned.1.call-start = ((), (), s32[]{:S(2)}) async-start(), calls=%async_computation.4 | async-start | bytes 8519680 | tf_op jit(solution)/shard_map/reduce_scatter | solution.py:88
  281.2 491.2 %copy-start.1 = (bf16[1,32,1024]{2,1,0:T(8,128)(2,1)S(1)}, bf16[1,32,1024]{2,1,0:T(8,128)(2,1)}, u32[]{:S(2)}) copy-start(bf16[1,32,1024]{2,1,0:T(8,128)(2,1)} %param.17) | copy-start | bytes 196612
  281.2 491.2 %copy-start.3 = (f32[32,2048]{1,0:T(8,128)S(1)}, f32[32,2048]{1,0:T(8,128)}, u32[]{:S(2)}) copy-start(f32[32,2048]{1,0:T(8,128)} %copy-done.2) | copy-start | bytes 786436
  281.2 491.2 %all-gather.12.cloned.1.call-start = ((), (), s32[]{:S(2)}) async-start(), calls=%async_computation.5 | async-start | bytes 2621440 | tf_op jit(solution)/shard_map/all_gather | solution.py:92
Sparse Core Ops, SparseCore 0:
  9.2 50.2 all-gather.5
  61.3 50.1 all-gather.9
  115.2 129.6 all-gather.7
  281.4 466.6 reduce-scatter.1
  749.7 22.7 all-gather.11
where the time goes:
time: 786 us; the launch traced here: 782 us
  waiting for transfers between devices  683 us (87%)
  local copies, waits for them, and re-layouts  33.4 us (4%)
  blocking collectives  25.5 us (3%)
  between operations  15.1 us (2%)
  matrix products  10.9 us (1%)
  other arithmetic  8.46 us (1%)
    reduce_scatter x1, waiting for transfers between devices, local(): lax.psum_scatter(result.reshape(count, width), 'seq', scatter_dimension=0...  466 us
    all_gather x1, waiting for transfers between devices, local(): lax.all_gather(queries, 'seq', axis=0, tiled=True)  126 us
    all_gather x1, waiting for transfers between devices, local(): lax.all_gather(w_qu, 'user', axis=0, tiled=True)  49.4 us
    all_gather x1, blocking collectives, local(): lax.all_gather(slot_cand[0], 'seq', axis=0, tiled=True)  25.5 us
    all_gather x1, waiting for transfers between devices, local(): lax.all_gather(w_o, 'user', axis=0, tiled=True)  21.3 us
    all_gather x1, waiting for transfers between devices, local(): lax.all_gather(w_kv, 'user', axis=0, tiled=True)  18 us
  transfers between devices with their start and end apart: 5, of which 5 were waited for; matrix products, arithmetic and copies ran while one was open for 2% of the time, Pallas kernels for 0%

commit v1 on v0

v1 whole, which is shorter than its diff:
```python
import jax
import jax.numpy as jnp
from jax import lax
from jax.experimental import pallas as pl
from jax.experimental.pallas import tpu as pltpu
from jax.sharding import PartitionSpec as P

MESH = pl.DeviceIdType.MESH
F32 = jnp.float32
BF16 = jnp.bfloat16

NX, NY, NZ = 4, 2, 8
SLOTS = 32
OWN = NX * NY
ROWS = OWN * SLOTS
WIDTH = 1024
WIDE = 256
GROUPS = WIDTH // WIDE
HEADS = 8
HEAD = 32
SPAN = 512
KBLK = 128
BLOCKS = SPAN // KBLK
CB = 128
STEPS = 16
QUARTER = 256


def silu(v):
    half = 0.5 * v
    return half + half * jnp.tanh(half)


def normed(rows):
    rows = rows.astype(F32)
    center = rows - jnp.mean(rows, axis=-1, keepdims=True)
    spread = jnp.mean(center * center, axis=-1, keepdims=True)
    return center * lax.rsqrt(spread + 1e-05)


def kernel(
    len_ref, start_ref, slot_ref, hist_ref, cand_ref, wkv_hbm, wqu_hbm, wo_hbm, out_ref,
    wq, wkv, wg, wo, nhist, ncand, gates, keys, vals, qall, masks,
    st1, st2, part, ra, sb, rb, sc, rc, keep, sd, rd,
    w_send, w_recv, w_local, st_send, st1_recv, st2_recv, q_send, q_recv,
    ring_send, ring_recv, a_send, a_recv, b_send, b_recv, c_send, c_recv, d_send, d_recv,
):
    seq = lax.axis_index("seq")
    user = lax.axis_index("user")
    yh = lax.div(seq, NZ * NX)
    z = lax.rem(lax.div(seq, NX), NZ)
    x = lax.rem(seq, NX)
    yl = lax.div(user, 2)
    core = lax.rem(user, 2)
    owner = x * NY + yh

    def seq_of(y_, z_, x_):
        return y_ * (NZ * NX) + z_ * NX + x_

    x_next, x_prev, x_far = lax.rem(x + 1, NX), lax.rem(x + 3, NX), lax.rem(x + 2, NX)
    sib_user = user + 1 - 2 * core
    opp_user = (1 - yl) * 2 + core
    sibling = (seq, sib_user)
    near = (seq, opp_user)
    cross = (seq_of(1 - yh, z, x), opp_user)
    right_x = (seq_of(yh, z, x_next), user)
    left_x = (seq_of(yh, z, x_prev), user)
    mirror = (seq_of(1 - yh, z, x), user)
    up_z = (seq_of(yh, lax.rem(z + 1, NZ), x), user)
    down_z = (seq_of(yh, lax.rem(z + NZ - 1, NZ), x), user)
    flat = []
    for dx in range(NX):
        for dy in range(NY):
            if dx or dy:
                px, py = lax.rem(x + dx, NX), lax.rem(yh + dy, NY)
                flat.append(((seq_of(py, z, px), user), px * NY + py))
    column = []
    for dz in range(1, NZ):
        pz = lax.rem(z + dz, NZ)
        column.append(((seq_of(yh, pz, x), user), pz))

    barrier = pltpu.get_barrier_semaphore()
    peers = [sibling, near, cross] + [p for p, _ in flat] + [p for p, _ in column]
    for peer in peers:
        pl.semaphore_signal(barrier, inc=1, device_id=peer, device_id_type=MESH)
    pl.semaphore_wait(barrier, len(peers))

    def remote(src, dst, send, recv, device):
        return pltpu.make_async_remote_copy(
            src_ref=src, dst_ref=dst, send_sem=send, recv_sem=recv, device_id=device, device_id_type=MESH
        )

    pieces = (
        (wqu_hbm, 0, WIDTH, wq),
        (wkv_hbm, 0, 2 * WIDTH, wkv),
        (wqu_hbm, WIDTH, WIDTH, wg),
        (wo_hbm, 0, WIDTH, wo),
    )

    def own_rows(index):
        return pl.ds(pl.multiple_of(index * QUARTER, QUARTER), QUARTER)

    def w_copy(n, kind):
        hbm, lo, cols, dst = pieces[n]
        half = cols // 2
        if kind == 0:
            return remote(hbm.at[:, pl.ds(lo, cols)], dst.at[own_rows(user), :], w_send.at[n, 0], w_recv.at[n, 0], sibling)
        if kind in (1, 2):
            shift = (kind - 1) * half
            return remote(
                hbm.at[:, pl.ds(lo + shift, half)], dst.at[own_rows(user), pl.ds(shift, half)],
                w_send.at[n, kind], w_recv.at[n, kind], near if kind == 1 else cross,
            )
        shift = (kind - 3) * half
        ref = dst.at[own_rows(opp_user), pl.ds(shift, half)]
        return remote(ref, ref, w_send.at[n, kind], w_recv.at[n, kind], sibling)

    def w_mine(n):
        hbm, lo, cols, dst = pieces[n]
        return pltpu.make_async_copy(hbm.at[:, pl.ds(lo, cols)], dst.at[own_rows(user), :], w_local.at[n])

    def w_start(n):
        for kind in (1, 2, 0):
            w_copy(n, kind).start()
        w_mine(n).start()

    def w_arrived(n, kind):
        _, _, cols, dst = pieces[n]
        half = cols // 2
        if kind == 0:
            ref = dst.at[own_rows(sib_user), :]
        elif kind in (1, 2):
            ref = dst.at[own_rows(opp_user), pl.ds((kind - 1) * half, half)]
        else:
            ref = dst.at[own_rows((1 - yl) * 2 + 1 - core), pl.ds((kind - 3) * half, half)]
        remote(ref, ref, w_send.at[n, kind], w_recv.at[n, kind], sibling).wait_recv()

    def w_forward(n):
        for kind in (1, 2):
            w_arrived(n, kind)
            w_copy(n, kind + 2).start()

    def w_finish(n):
        w_mine(n).wait()
        w_arrived(n, 0)
        w_arrived(n, 3)
        w_arrived(n, 4)

    def w_sent(n, kinds):
        for kind in kinds:
            w_copy(n, kind).wait_send()

    w_start(0)

    slots = slot_ref[...]
    window = jnp.zeros(slots.shape, F32)
    for c in range(start_ref.shape[1]):
        begin = start_ref[0, c].astype(F32)
        window = window + jnp.where((slots >= c * CB) & (slots < (c + 1) * CB), begin, 0.0)
    st1[owner] = jnp.zeros((8, 128), F32)
    st1[owner, 0:1, 0:SLOTS] = window
    for n, (peer, _) in enumerate(flat):
        remote(st1.at[owner], st1.at[owner], st_send.at[0, n], st1_recv.at[owner], peer).start()

    ncand[...] = normed(cand_ref[...]).astype(BF16)

    def clear(n, carry):
        keys[lax.div(n, BLOCKS), lax.rem(n, BLOCKS)] = jnp.zeros((WIDE, HEADS * KBLK), BF16)
        vals[lax.div(n, BLOCKS), lax.rem(n, BLOCKS)] = jnp.zeros((HEADS * KBLK, WIDE), BF16)
        return carry

    lax.fori_loop(0, GROUPS * BLOCKS, clear, 0)

    for n, (peer, o) in enumerate(flat):
        remote(st1.at[o], st1.at[o], st_send.at[0, n], st1_recv.at[o], peer).wait_recv()
    st2[z] = jnp.concatenate([st1[o, 0:1, :] for o in range(OWN)], axis=0)
    for n, (peer, _) in enumerate(column):
        remote(st2.at[z], st2.at[z], st_send.at[1, n], st2_recv.at[z], peer).start()

    w_sent(0, (1, 2))
    w_start(1)
    w_forward(0)
    w_finish(0)

    queries = silu(jnp.dot(ncand[...], wq[...], preferred_element_type=F32)).astype(BF16)
    mine = pl.ds(pl.multiple_of(owner * SLOTS, SLOTS), SLOTS)
    for g in range(GROUPS):
        qall[z, g, mine, :] = queries[:, g * WIDE:(g + 1) * WIDE]
    for n, (peer, _) in enumerate(flat):
        ref = qall.at[z, :, mine, :]
        remote(ref, ref, q_send.at[n], q_recv.at[owner], peer).start()

    def norm_rows(n, carry):
        rows = pl.ds(pl.multiple_of(n * 64, 64), 64)
        nhist[rows, :] = normed(hist_ref[rows, :]).astype(BF16)
        return carry

    lax.fori_loop(0, SPAN // 64, norm_rows, 0)

    for n, (peer, pz) in enumerate(column):
        remote(st2.at[pz], st2.at[pz], st_send.at[1, n], st2_recv.at[pz], peer).wait_recv()
    lane = lax.broadcasted_iota(jnp.int32, (SLOTS, 128), 1)
    line = lax.broadcasted_iota(jnp.int32, (SLOTS, 128), 0)
    first = (seq * BLOCKS).astype(F32)

    def make_masks(n, carry):
        tile = st2[n]
        for o in range(OWN):
            spread = jnp.broadcast_to(tile[o:o + 1, :], (SLOTS, 128))
            begin = jnp.sum(jnp.where(lane == line, spread, 0.0), axis=1, keepdims=True)
            begin = jnp.broadcast_to(begin, (SLOTS, 128))
            for j in range(BLOCKS):
                masks[n, j, o * SLOTS:(o + 1) * SLOTS, :] = jnp.where(begin <= first + j, 1.0, 0.0).astype(BF16)
        return carry

    lax.fori_loop(0, NZ, make_masks, 0)

    for n, (peer, o) in enumerate(flat):
        ref = qall.at[z, :, pl.ds(pl.multiple_of(o * SLOTS, SLOTS), SLOTS), :]
        remote(ref, ref, q_send.at[n], q_recv.at[o], peer).wait_recv()

    def ring(side, index, z_of, g):
        ref = qall.at[z_of, g]
        return remote(ref, ref, ring_send.at[side, index], ring_recv.at[side, index], up_z if side == 0 else down_z)

    for g in range(GROUPS):
        ring(0, g, z, g).start()
        ring(1, g, z, g).start()

    w_sent(1, (1, 2))
    w_start(2)
    w_forward(1)
    w_finish(1)

    place = lax.broadcasted_iota(jnp.int32, (SPAN, WIDE), 0) + seq * SPAN
    exists = jnp.where(place < len_ref[0], 0.5, 0.0)
    spot = lax.broadcasted_iota(jnp.int32, (KBLK, 128), 1)
    for g in range(GROUPS):
        k = silu(jnp.dot(nhist[...], wkv[:, g * WIDE:(g + 1) * WIDE], preferred_element_type=F32))
        k = k.astype(BF16).astype(F32) * exists
        kt = k.T.astype(BF16)
        for j in range(BLOCKS):
            for h in range(HEADS):
                keys[g, j, h * HEAD:(h + 1) * HEAD, h * KBLK:(h + 1) * KBLK] = (
                    kt[h * HEAD:(h + 1) * HEAD, j * KBLK:(j + 1) * KBLK]
                )
        v = silu(jnp.dot(nhist[...], wkv[:, WIDTH + g * WIDE:WIDTH + (g + 1) * WIDE], preferred_element_type=F32))
        for j in range(BLOCKS):
            for h in range(HEADS):
                side, at = (h * HEAD) // 128 * 128, (h * HEAD) % 128
                own = v[j * KBLK:(j + 1) * KBLK, side:side + 128]
                own = jnp.where((spot >= at) & (spot < at + HEAD), own, 0.0).astype(BF16)
                vals[g, j, h * KBLK:(h + 1) * KBLK, side:side + 128] = own

    def piece(it, side):
        ahead = lax.div(STEPS - 1 - it, STEPS - 1)
        last = lax.div(it, STEPS - 1)
        mid = 1 - ahead - last
        k = it - 1 + ahead - last
        hop = mid * (1 + lax.div(k, GROUPS))
        if side == 0:
            return lax.rem(z + NZ - hop, NZ), mid * lax.rem(k, GROUPS) + 2 * last
        return lax.rem(z + hop, NZ), mid * (lax.rem(k, GROUPS) + 2 * lax.div(k, 12)) + ahead + 3 * last

    def attend(z_of, g, p):
        total = jnp.zeros((ROWS, WIDE), F32)
        for j in range(BLOCKS):
            mask = masks[z_of, j]
            q = qall[z_of, g] * jnp.concatenate([mask, mask], axis=1)
            for i in range(4):
                cols = slice(i * WIDE, (i + 1) * WIDE)
                s = jnp.dot(q, keys[g, j, :, cols], preferred_element_type=F32)
                w = (s + s * jnp.tanh(s)).astype(BF16)
                total = total + jnp.dot(w, vals[g, j, cols, :], preferred_element_type=F32)
        part[p] = total.astype(BF16)

    def x_rows(x_of):
        return pl.ds(pl.multiple_of(x_of * (NY * SLOTS), NY * SLOTS), NY * SLOTS)

    def a_copy(p, side):
        lanes = pl.ds(side * 128, 128)
        return remote(
            part.at[p, x_rows(x_far), lanes], ra.at[side, p], a_send.at[side, p], a_recv.at[side, p],
            right_x if side == 0 else left_x,
        )

    def b_copy(p, side):
        return remote(
            sb.at[side, p], rb.at[side, p], b_send.at[side, p], b_recv.at[side, p], right_x if side == 0 else left_x
        )

    def c_copy(p):
        return remote(sc.at[p], rc.at[p], c_send.at[p], c_recv.at[p], mirror)

    def d_copy(p, z_of, g):
        return remote(sd.at[p], rd.at[z, g], d_send.at[p], d_recv.at[z, g], (seq_of(yh, z_of, x), user))

    def stage_b(it):
        for s in range(2):
            p = 2 * it + s
            for side in range(2):
                a_copy(p, side).wait()
                toward = x_next if side == 0 else x_prev
                sb[side, p] = part[p, x_rows(toward), :]
                lanes = slice(side * 128, side * 128 + 128)
                own = part[p, x_rows(toward), lanes].astype(F32) + ra[side, p].astype(F32)
                sb[side, p, :, lanes] = own.astype(BF16)
                b_copy(p, side).start()

    def stage_c(it):
        for s in range(2):
            p = 2 * it + s
            b_copy(p, 0).wait()
            b_copy(p, 1).wait()

            def some(y_of):
                rows = pl.ds(pl.multiple_of(y_of * SLOTS, SLOTS), SLOTS)
                at = pl.ds(pl.multiple_of(x * (NY * SLOTS) + y_of * SLOTS, SLOTS), SLOTS)
                return part[p, at, :].astype(F32) + rb[0, p, rows, :].astype(F32) + rb[1, p, rows, :].astype(F32)

            sc[p] = some(1 - yh).astype(BF16)
            c_copy(p).start()
            keep[p] = some(yh)

    def stage_d(it, own):
        for s in range(2):
            p = 2 * it + s
            c_copy(p).wait()
            total = keep[p] + rc[p].astype(F32)
            z_of, g = piece(it, s)
            if own:
                rd[z, g] = total.astype(BF16)
            else:
                sd[p] = total.astype(BF16)
                d_copy(p, z_of, g).start()

    def step(it, carry):
        k = it - 1

        @pl.when((it >= 1) & (it < STEPS - 1))
        def _():
            for side in range(2):
                z_of, g = piece(it, side)
                ring(side, k, z_of, g).wait_recv()

        @pl.when((it >= 1) & (k < 10))
        def _():
            z_of, g = piece(it, 0)
            ring(0, k + 4, z_of, g).start()

        @pl.when((it >= 1) & (k < 8))
        def _():
            z_of, g = piece(it, 1)
            ring(1, k + 4, z_of, g).start()

        @pl.when((k == 10) | (k == 11))
        def _():
            z_of, g = piece(it, 1)
            ring(1, k + 2, z_of, g).start()

        @pl.when(it >= 2)
        def _():
            stage_b(it - 2)

        @pl.when(it >= 3)
        def _():
            stage_c(it - 3)

        @pl.when(it == 4)
        def _():
            stage_d(0, True)

        @pl.when(it >= 5)
        def _():
            stage_d(it - 4, False)

        @pl.when(it == 4)
        def _():
            w_sent(2, (1, 2))
            w_start(3)
            w_forward(2)

        @pl.when(it == 8)
        def _():
            w_forward(3)

        for side in range(2):
            z_of, g = piece(it, side)
            attend(z_of, g, 2 * it + side)
            a_copy(2 * it + side, 0).start()
            a_copy(2 * it + side, 1).start()
        return carry

    lax.fori_loop(0, STEPS, step, 0)

    stage_b(STEPS - 2)
    stage_c(STEPS - 3)
    stage_d(STEPS - 4, False)
    w_finish(2)
    w_finish(3)
    gates[...] = silu(jnp.dot(ncand[...], wg[...], preferred_element_type=F32))
    stage_b(STEPS - 1)
    stage_c(STEPS - 2)
    stage_d(STEPS - 3, False)
    stage_c(STEPS - 1)
    stage_d(STEPS - 2, False)
    stage_d(STEPS - 1, True)

    for _, pz in column:
        for g in range(GROUPS):
            remote(sd.at[0], rd.at[pz, g], d_send.at[0], d_recv.at[pz, g], sibling).wait_recv()
    mixed = jnp.concatenate(
        [sum(rd[n, g].astype(F32) for n in range(NZ)) for g in range(GROUPS)], axis=1
    )
    gated = (normed(mixed).astype(BF16).astype(F32) * gates[...]).astype(BF16)
    projected = jnp.dot(gated, wo[...], preferred_element_type=F32)
    out_ref[...] = (cand_ref[...].astype(F32) + projected).astype(BF16)

    w_sent(0, (0, 3, 4))
    w_sent(1, (0, 3, 4))
    w_sent(2, (0, 3, 4))
    w_sent(3, (0, 1, 2, 3, 4))
    for n, (peer, _) in enumerate(flat):
        remote(st1.at[owner], st1.at[owner], st_send.at[0, n], st1_recv.at[owner], peer).wait_send()
        ref = qall.at[z, :, mine, :]
        remote(ref, ref, q_send.at[n], q_recv.at[owner], peer).wait_send()
    for n, (peer, _) in enumerate(column):
        remote(st2.at[z], st2.at[z], st_send.at[1, n], st2_recv.at[z], peer).wait_send()

    def ring_sent(n, carry):
        for side in range(2):
            ring(side, n, z, 0).wait_send()
        return carry

    lax.fori_loop(0, 14, ring_sent, 0)

    def d_sent(n, carry):
        remote(sd.at[n], rd.at[z, 0], d_send.at[n], d_recv.at[z, 0], sibling).wait_send()
        return carry

    lax.fori_loop(2, 2 * STEPS - 2, d_sent, 0)


def local(history, hist_len, cand_start, candidates, slot_cand, w_kv, w_qu, w_o):
    pieces = 2 * STEPS
    vmem = pl.BlockSpec(memory_space=pltpu.VMEM)
    smem = pl.BlockSpec(memory_space=pltpu.SMEM)
    anywhere = pl.BlockSpec(memory_space=pl.ANY)
    dma = pltpu.SemaphoreType.DMA
    out = pl.pallas_call(
        kernel,
        out_shape=jax.ShapeDtypeStruct((SLOTS, WIDTH), BF16),
        in_specs=[smem, smem, vmem, vmem, vmem, anywhere, anywhere, anywhere],
        out_specs=vmem,
        scratch_shapes=[
            pltpu.VMEM((WIDTH, WIDTH), BF16),
            pltpu.VMEM((WIDTH, 2 * WIDTH), BF16),
            pltpu.VMEM((WIDTH, WIDTH), BF16),
            pltpu.VMEM((WIDTH, WIDTH), BF16),
            pltpu.VMEM((SPAN, WIDTH), BF16),
            pltpu.VMEM((SLOTS, WIDTH), BF16),
            pltpu.VMEM((SLOTS, WIDTH), F32),
            pltpu.VMEM((GROUPS, BLOCKS, WIDE, HEADS * KBLK), BF16),
            pltpu.VMEM((GROUPS, BLOCKS, HEADS * KBLK, WIDE), BF16),
            pltpu.VMEM((NZ, GROUPS, ROWS, WIDE), BF16),
            pltpu.VMEM((NZ, BLOCKS, ROWS, 128), BF16),
            pltpu.VMEM((OWN, 8, 128), F32),
            pltpu.VMEM((NZ, 8, 128), F32),
            pltpu.VMEM((pieces, ROWS, WIDE), BF16),
            pltpu.VMEM((2, pieces, NY * SLOTS, 128), BF16),
            pltpu.VMEM((2, pieces, NY * SLOTS, WIDE), BF16),
            pltpu.VMEM((2, pieces, NY * SLOTS, WIDE), BF16),
            pltpu.VMEM((pieces, SLOTS, WIDE), BF16),
            pltpu.VMEM((pieces, SLOTS, WIDE), BF16),
            pltpu.VMEM((pieces, SLOTS, WIDE), F32),
            pltpu.VMEM((pieces, SLOTS, WIDE), BF16),
            pltpu.VMEM((NZ, GROUPS, SLOTS, WIDE), BF16),
            dma((4, 5)), dma((4, 5)), dma((4,)),
            dma((2, 7)), dma((OWN,)), dma((NZ,)),
            dma((7,)), dma((OWN,)),
            dma((2, 14)), dma((2, 14)),
            dma((2, pieces)), dma((2, pieces)),
            dma((2, pieces)), dma((2, pieces)),
            dma((pieces,)), dma((pieces,)),
            dma((pieces,)), dma((NZ, GROUPS)),
        ],
        compiler_params=pltpu.CompilerParams(
            collective_id=0, has_side_effects=True, vmem_limit_bytes=60 * 2**20
        ),
    )(hist_len, cand_start, slot_cand, history[0], candidates[0], w_kv, w_qu, w_o)
    return out[None]


def solution(mesh):
    in_specs = (
        P("user", "seq", None),
        P("user"),
        P("user", None),
        P("user", "seq", None),
        P("user", "seq"),
        P("user", None),
        P("user", None),
        P("user", None),
    )
    out_specs = P("user", "seq", None)
    return jax.shard_map(local, mesh=mesh, in_specs=in_specs, out_specs=out_specs, check_vma=False)
```

time: 786 us -> 122 us (0.16)
  waiting for transfers between devices: 683 us -> 0 us
  Pallas kernels: 0 us -> 120 us
  local copies, waits for them, and re-layouts: 33.4 us -> 1.47 us
  blocking collectives: 25.5 us -> 0 us
  between operations: 15.1 us -> 0.66 us
  matrix products: 10.9 us -> 0 us
  other arithmetic: 8.46 us -> 0 us
    reduce_scatter x1 -> x0, waiting for transfers between devices: 466 us -> none  [local(): lax.psum_scatter(result.reshape(count, width), 'seq', scatter_dimension=0...]
    all_gather x4 -> x0, waiting for transfers between devices: 215 us -> none  [the longest x1 126 us: local(): lax.all_gather(queries, 'seq', axis=0, tiled=True)]
    pallas_call x0 -> x1, Pallas kernels: none -> 120 us  [local(): pl.pallas_call(kernel, out_shape=jax.ShapeDtypeStruct((SLOTS, WIDTH), BF1...]
    all_gather x1 -> x0, blocking collectives: 25.5 us -> none  [local(): lax.all_gather(slot_cand[0], 'seq', axis=0, tiled=True)]
    dynamic_update_slice x8 -> x0, local copies, waits for them, and re-layouts: 13.6 us -> none  [local(): lax.map(lambda items: partial_rows(items[0], items[1]), (q_blocks, low_bl...]
    dot_general x3 -> x0, matrix products: 10.9 us -> none  [the longest x1 5.09 us: local(): jnp.dot(normed_hist, lax.all_gather(w_kv, 'user', axis=0, tiled=True), pr...]
    while x3 -> x0, local copies, waits for them, and re-layouts: 8.09 us -> none  [local(): lax.map(lambda items: partial_rows(items[0], items[1]), (q_blocks, low_bl...]
  transfers between devices with their start and end apart: 5 -> 0, of which waited for: 5 -> 0; matrix products, arithmetic and copies ran while one was open for 2% -> 0% of each run, Pallas kernels for 0% -> 0%
where the time goes in v1:
time: 122 us
  Pallas kernels  120 us (98%)
  local copies, waits for them, and re-layouts  1.47 us (1%)
    pallas_call x1, Pallas kernels, local(): pl.pallas_call(kernel, out_shape=jax.ShapeDtypeStruct((SLOTS, WIDTH), BF1...  120 us

profile of v1, /device:TPU:8, one launch (start us, length us, event | category | flops | bytes accessed | tf_op | source)
XLA Modules:
  0.0 121.7 jit_solution(18112099566028933889)
XLA Ops:
  0.7 119.5 %shard_map.82 = bf16[32,1024]{1,0:T(8,128)(2,1)} custom-call(s32[1]{0:T(128)S(6)} %copy.10.len_ref, s32[1,16]{1,0:T(1,128)} %start_ref.1, s32[1,32]{1,0:T(1,128)} %slot_ref.1, bf16[512,1024]{1,0:T(8,128)(2,1)} %bitcast.3, bf16[32,1024]{1,0:T(8,128)(2,1)} %bitcast.5, bf16[256,2048]{1,0:T(8,128)(2,1)} %wkv_hbm.1, bf16[256,2048]{1,0:T(8,128)(2,1)} %wqu_hbm.1, ...), custom_call_target="tpu_custom_call" | custom-call | tf_op jit(solution)/shard_map/pallas_call | solution.py:450
  120.2 1.5 %copy.11 = bf16[1,32,1024]{2,1,0:T(8,128)(2,1)} copy(bf16[1,32,1024]{2,1,0:T(8,128)(2,1)} %bitcast.4) | data formatting | bytes 131072

commit v2 on v1

v2 whole, which is shorter than its diff:
```python
import jax
import jax.numpy as jnp
from jax import lax
from jax.experimental import pallas as pl
from jax.experimental.pallas import tpu as pltpu
from jax.sharding import PartitionSpec as P

MESH = pl.DeviceIdType.MESH
F32 = jnp.float32
BF16 = jnp.bfloat16

NX, NY, NZ = 4, 2, 8
SLOTS = 32
OWN = NX * NY
ROWS = OWN * SLOTS
WIDTH = 1024
WIDE = 256
GROUPS = WIDTH // WIDE
HEADS = 8
HEAD = 32
SPAN = 512
KBLK = 128
BLOCKS = SPAN // KBLK
CB = 128
STEPS = 16
CUT = 12
LAG = 4
QUARTER = 256


def silu(v):
    half = 0.5 * v
    return half + half * jnp.tanh(half)


def normed(rows):
    rows = rows.astype(F32)
    center = rows - jnp.mean(rows, axis=-1, keepdims=True)
    spread = jnp.mean(center * center, axis=-1, keepdims=True)
    return center * lax.rsqrt(spread + 1e-05)


def kernel(
    len_ref, start_ref, slot_ref, hist_ref, cand_ref, wkv_hbm, wqu_hbm, wo_hbm, out_ref,
    wqu, wkv, wo, nhist, ncand, cin, pq, pg, rq, rg, keys, vals, qall, masks,
    st1, st2, part, dr, sc, keep, sd, rd, rown,
    w_send, w_recv, w_local, p_send, p_recv, p_local, st_send, st1_recv, st2_recv, q_send, q_recv,
    ring_send, ring_recv, x_send, x_recv, y_send, y_recv, d_send, d_recv,
):
    seq = lax.axis_index("seq")
    user = lax.axis_index("user")
    yh = lax.div(seq, NZ * NX)
    z = lax.rem(lax.div(seq, NX), NZ)
    x = lax.rem(seq, NX)
    yl = lax.div(user, 2)
    core = lax.rem(user, 2)
    owner = x * NY + yh

    def seq_of(y_, z_, x_):
        return y_ * (NZ * NX) + z_ * NX + x_

    sib_user = user + 1 - 2 * core
    opp_user = (1 - yl) * 2 + core
    sibling = (seq, sib_user)
    near = (seq, opp_user)
    cross = (seq_of(1 - yh, z, x), opp_user)
    mirror = (seq_of(1 - yh, z, x), user)
    opposite = [(s_, (1 - yl) * 2 + k) for s_ in (seq, seq_of(1 - yh, z, x)) for k in range(2)]
    up_z = (seq_of(yh, lax.rem(z + 1, NZ), x), user)
    down_z = (seq_of(yh, lax.rem(z + NZ - 1, NZ), x), user)
    row = []
    for dx in range(1, NX):
        px = lax.rem(x + dx, NX)
        row.append(((seq_of(yh, z, px), user), px))
    flat = []
    for dx in range(NX):
        for dy in range(NY):
            if dx or dy:
                px, py = lax.rem(x + dx, NX), lax.rem(yh + dy, NY)
                flat.append(((seq_of(py, z, px), user), px * NY + py))
    column = []
    for dz in range(1, NZ):
        pz = lax.rem(z + dz, NZ)
        column.append(((seq_of(yh, pz, x), user), pz))

    barrier = pltpu.get_barrier_semaphore()
    peers = [sibling] + opposite + [p for p, _ in flat] + [p for p, _ in column]
    for peer in peers:
        pl.semaphore_signal(barrier, inc=1, device_id=peer, device_id_type=MESH)

    slots = slot_ref[...]
    window = jnp.zeros(slots.shape, F32)
    for c in range(start_ref.shape[1]):
        begin = start_ref[0, c].astype(F32)
        window = window + jnp.where((slots >= c * CB) & (slots < (c + 1) * CB), begin, 0.0)
    st1[owner] = jnp.zeros((8, 128), F32)
    st1[owner, 0:1, 0:SLOTS] = window
    pltpu.make_async_copy(wqu_hbm, wqu, p_local).start()
    rows = normed(cand_ref[...]).astype(BF16)
    for u in range(4):
        ncand[u] = rows[:, u * QUARTER:(u + 1) * QUARTER]
    cin[0:SLOTS, :] = ncand[user]

    def clear(n, carry):
        keys[lax.div(n, BLOCKS), lax.rem(n, BLOCKS)] = jnp.zeros((WIDE, HEADS * KBLK), BF16)
        vals[lax.div(n, BLOCKS), lax.rem(n, BLOCKS)] = jnp.zeros((HEADS * KBLK, WIDE), BF16)
        return carry

    lax.fori_loop(0, GROUPS * BLOCKS, clear, 0)
    pl.semaphore_wait(barrier, len(peers))

    def remote(src, dst, send, recv, device):
        return pltpu.make_async_remote_copy(
            src_ref=src, dst_ref=dst, send_sem=send, recv_sem=recv, device_id=device, device_id_type=MESH
        )

    def halves(hbm, lo, cols, dst):
        return tuple((hbm, lo + s * (cols // 2), dst, s * (cols // 2), cols // 2) for s in range(2))

    pieces = []
    for g in range(GROUPS):
        pieces.append(tuple((wkv_hbm, s * WIDTH + g * WIDE, wkv, s * WIDTH + g * WIDE, WIDE) for s in range(2)))
    pieces += [halves(wo_hbm, 0, WIDTH, wo)]
    W_OUT = GROUPS

    def own_rows(index):
        return pl.ds(pl.multiple_of(index * QUARTER, QUARTER), QUARTER)

    def w_copy(n, kind):
        hbm, lo, dst, at, cols = pieces[n][kind % 2]
        sems = (w_send.at[n, kind], w_recv.at[n, kind])
        if kind < 4:
            target = (near, cross, sibling, sibling)[kind]
            return remote(hbm.at[:, pl.ds(lo, cols)], dst.at[own_rows(user), pl.ds(at, cols)], *sems, target)
        ref = dst.at[own_rows(opp_user), pl.ds(at, cols)]
        return remote(ref, ref, *sems, sibling)

    def w_mine(n, s):
        hbm, lo, dst, at, cols = pieces[n][s]
        return pltpu.make_async_copy(hbm.at[:, pl.ds(lo, cols)], dst.at[own_rows(user), pl.ds(at, cols)], w_local.at[n, s])

    def w_start(n):
        for kind in range(4):
            w_copy(n, kind).start()
        for s in range(2):
            w_mine(n, s).start()

    def w_arrived(n, kind):
        _, _, dst, at, cols = pieces[n][kind % 2]
        rows = (opp_user, sib_user, (1 - yl) * 2 + 1 - core)[kind // 2]
        ref = dst.at[own_rows(rows), pl.ds(at, cols)]
        remote(ref, ref, w_send.at[n, kind], w_recv.at[n, kind], sibling).wait_recv()

    def w_forward(n):
        for kind in (0, 1):
            w_arrived(n, kind)
            w_copy(n, kind + 4).start()

    def w_finish(n):
        for s in range(2):
            w_mine(n, s).wait()
        for kind in range(2, 6):
            w_arrived(n, kind)

    def w_sent(n, kinds):
        for kind in kinds:
            w_copy(n, kind).wait_send()

    half = SLOTS // 2
    near_at = pl.ds(pl.multiple_of(2 * SLOTS + half * core, half), half)
    cross_at = pl.ds(pl.multiple_of(3 * SLOTS + half * core, half), half)

    def in_copy(n):
        if n == 0:
            return remote(ncand.at[sib_user], cin.at[pl.ds(SLOTS, SLOTS), :], p_send.at[0, 0], p_recv.at[0, 0], sibling)
        far, k = divmod(n - 1, 2)
        return remote(
            ncand.at[(1 - yl) * 2 + k, pl.ds(far * half, half), :], cin.at[cross_at if far else near_at, :],
            p_send.at[0, n], p_recv.at[0, 1 + 2 * far + core], opposite[n - 1],
        )

    def in_arrived(n):
        size = SLOTS if n == 0 else half
        ref = cin.at[pl.ds(0 if n == 0 else 2 * SLOTS, size), :]
        remote(ref, ref, p_send.at[0, n], p_recv.at[0, n], sibling).wait_recv()

    def back_copy(m, n):
        src, dst = ((pq, rq), (pg, rg))[m - 1]
        if n == 0:
            return remote(src.at[pl.ds(SLOTS, SLOTS), :], dst.at[0], p_send.at[m, 0], p_recv.at[m, 0], sibling)
        far, k = divmod(n - 1, 2)
        return remote(
            src.at[pl.ds((2 + far) * SLOTS + k * half, half), :], dst.at[1 + core, pl.ds(far * half, half), :],
            p_send.at[m, n], p_recv.at[m, 1 + 2 * far + core], opposite[n - 1],
        )

    def back_arrived(m, n):
        dst = (rq, rg)[m - 1]
        ref = dst.at[0] if n == 0 else dst.at[1, pl.ds(0, half), :]
        remote(ref, ref, p_send.at[m, n], p_recv.at[m, n], sibling).wait_recv()

    for n in range(5):
        in_copy(n).start()
    w_start(0)
    w_start(1)
    for n, (peer, _) in enumerate(flat):
        remote(st1.at[owner], st1.at[owner], st_send.at[0, n], st1_recv.at[owner], peer).start()

    pltpu.make_async_copy(wqu_hbm, wqu, p_local).wait()
    for n in range(5):
        in_arrived(n)
    pq[...] = jnp.dot(cin[...], wqu[:, :WIDTH], preferred_element_type=F32)
    for n in range(5):
        back_copy(1, n).start()

    def norm_rows(n, carry):
        rows = pl.ds(pl.multiple_of(n * 64, 64), 64)
        nhist[rows, :] = normed(hist_ref[rows, :]).astype(BF16)
        return carry

    lax.fori_loop(0, SPAN // 64, norm_rows, 0)

    for n, (peer, o) in enumerate(flat):
        remote(st1.at[o], st1.at[o], st_send.at[0, n], st1_recv.at[o], peer).wait_recv()
    st2[z] = jnp.concatenate([st1[o, 0:1, :] for o in range(OWN)], axis=0)
    for n, (peer, _) in enumerate(column):
        remote(st2.at[z], st2.at[z], st_send.at[1, n], st2_recv.at[z], peer).start()

    w_sent(0, (0, 1))
    w_start(2)

    for n in range(5):
        back_arrived(1, n)
    queries = silu(pq[0:SLOTS, :] + rq[0] + rq[1] + rq[2]).astype(BF16)
    mine = pl.ds(pl.multiple_of(owner * SLOTS, SLOTS), SLOTS)

    def q_copy(g, n):
        ref = qall.at[z, g, mine, :]
        return remote(ref, ref, q_send.at[g], q_recv.at[g], flat[n][0])

    others = pl.ds(0, (OWN - 1) * SLOTS)

    def q_all(g):
        ref = qall.at[z, g, others, :]
        return remote(ref, ref, q_send.at[g], q_recv.at[g], mirror)

    for g in range(GROUPS):
        qall[z, g, mine, :] = queries[:, g * WIDE:(g + 1) * WIDE]
    for g in range(2):
        for n in range(OWN - 1):
            q_copy(g, n).start()

    def ring(side, index, z_of, g):
        ref = qall.at[z_of, g]
        return remote(ref, ref, ring_send.at[side, index], ring_recv.at[side, index], up_z if side == 0 else down_z)

    def ring_begin(g):
        q_all(g).wait_recv()
        ring(0, g, z, g).start()
        ring(1, g, z, g).start()

    def project(g):
        place = lax.broadcasted_iota(jnp.int32, (SPAN, WIDE), 0) + seq * SPAN
        exists = jnp.where(place < len_ref[0], 0.5, 0.0)
        spot = lax.broadcasted_iota(jnp.int32, (KBLK, 128), 1)
        k = silu(jnp.dot(nhist[...], wkv[:, g * WIDE:(g + 1) * WIDE], preferred_element_type=F32))
        k = k.astype(BF16).astype(F32) * exists
        kt = k.T.astype(BF16)
        for j in range(BLOCKS):
            for h in range(HEADS):
                keys[g, j, h * HEAD:(h + 1) * HEAD, h * KBLK:(h + 1) * KBLK] = (
                    kt[h * HEAD:(h + 1) * HEAD, j * KBLK:(j + 1) * KBLK]
                )
        v = silu(jnp.dot(nhist[...], wkv[:, WIDTH + g * WIDE:WIDTH + (g + 1) * WIDE], preferred_element_type=F32))
        for j in range(BLOCKS):
            for h in range(HEADS):
                side, at = (h * HEAD) // 128 * 128, (h * HEAD) % 128
                own = v[j * KBLK:(j + 1) * KBLK, side:side + 128]
                own = jnp.where((spot >= at) & (spot < at + HEAD), own, 0.0).astype(BF16)
                vals[g, j, h * KBLK:(h + 1) * KBLK, side:side + 128] = own

    w_forward(0)
    w_sent(1, (0, 1))
    w_start(3)
    w_forward(1)
    for g in range(2, GROUPS):
        for n in range(OWN - 1):
            q_copy(g, n).start()
    pg[...] = jnp.dot(cin[...], wqu[:, WIDTH:], preferred_element_type=F32)
    w_finish(0)
    project(0)
    for n, (peer, pz) in enumerate(column):
        remote(st2.at[pz], st2.at[pz], st_send.at[1, n], st2_recv.at[pz], peer).wait_recv()
    lane = lax.broadcasted_iota(jnp.int32, (SLOTS, 128), 1)
    line = lax.broadcasted_iota(jnp.int32, (SLOTS, 128), 0)
    first = (seq * BLOCKS).astype(F32)

    def make_masks(n, carry):
        tile = st2[n]
        for o in range(OWN):
            spread = jnp.broadcast_to(tile[o:o + 1, :], (SLOTS, 128))
            begin = jnp.sum(jnp.where(lane == line, spread, 0.0), axis=1, keepdims=True)
            begin = jnp.broadcast_to(begin, (SLOTS, 128))
            for j in range(BLOCKS):
                masks[n, j, o * SLOTS:(o + 1) * SLOTS, :] = jnp.where(begin <= first + j, 1.0, 0.0).astype(BF16)
        return carry

    lax.fori_loop(0, NZ, make_masks, 0)

    w_finish(1)
    project(1)
    ring_begin(0)
    ring_begin(1)

    def piece(it, side):
        ahead = lax.div(STEPS - 1 - it, STEPS - 1)
        last = lax.div(it, STEPS - 1)
        mid = 1 - ahead - last
        k = it - 1 + ahead - last
        hop = mid * (1 + lax.div(k, GROUPS))
        if side == 0:
            return lax.rem(z + NZ - hop, NZ), mid * lax.rem(k, GROUPS) + 2 * last
        return lax.rem(z + hop, NZ), mid * (lax.rem(k, GROUPS) + 2 * lax.div(k, 12)) + ahead + 3 * last

    def attend(z_of, g, p):
        total = jnp.zeros((ROWS, WIDE), F32)
        for j in range(BLOCKS):
            mask = masks[z_of, j]
            q = qall[z_of, g] * jnp.concatenate([mask, mask], axis=1)
            for i in range(4):
                cols = slice(i * WIDE, (i + 1) * WIDE)
                s = jnp.dot(q, keys[g, j, :, cols], preferred_element_type=F32)
                w = (s + s * jnp.tanh(s)).astype(BF16)
                total = total + jnp.dot(w, vals[g, j, cols, :], preferred_element_type=F32)
        part[p] = total.astype(BF16)

    def owner_rows(o):
        return pl.ds(pl.multiple_of(o * SLOTS, SLOTS), SLOTS)

    def places(n, count):
        return pl.ds(n * SLOTS, count * SLOTS)

    def first_copies(p, s):
        if s == 0:
            for n, (peer, px) in enumerate(row):
                rows = pl.ds(pl.multiple_of(px * (NY * SLOTS), NY * SLOTS), NY * SLOTS)
                remote(part.at[p, rows, :], dr.at[p, places(2 * n, 2), :], x_send.at[p], x_recv.at[p], peer).start()
        else:
            for n in range(NX):
                rows = owner_rows(n * NY + 1 - yh)
                remote(part.at[p, rows, :], dr.at[p, places(n, 1), :], x_send.at[p], x_recv.at[p], mirror).start()

    def first_all(p, s):
        ref = dr.at[p, places(0, (6, 4)[s]), :]
        return remote(ref, ref, x_send.at[p], x_recv.at[p], mirror)

    def second_copies(p, s):
        if s == 0:
            src = sc.at[p, places(0, 1), :]
            remote(src, dr.at[p, places(6, 1), :], y_send.at[p], y_recv.at[p], mirror).start()
        else:
            for n, (peer, _) in enumerate(row):
                src = sc.at[p, places(n, 1), :]
                remote(src, dr.at[p, places(4 + n, 1), :], y_send.at[p], y_recv.at[p], peer).start()

    def second_all(p, s):
        ref = dr.at[p, places(6, 1) if s == 0 else places(4, 3), :]
        return remote(ref, ref, y_send.at[p], y_recv.at[p], mirror)

    def o_copy(p, n):
        peer, o = flat[n]
        return remote(part.at[p, owner_rows(o), :], dr.at[p, pl.ds(n * SLOTS, SLOTS), :], x_send.at[p], x_recv.at[p], peer)

    def o_all(p):
        ref = dr.at[p]
        return remote(ref, ref, x_send.at[p], x_recv.at[p], mirror)

    def d_copy(p, z_of, g):
        hop = lax.rem(z + NZ - z_of, NZ) - 1
        return remote(sd.at[p], rd.at[hop, g], d_send.at[p], d_recv, (seq_of(yh, z_of, x), user))

    def deliver(it, s, total, own):
        p = 2 * it + s
        z_of, g = piece(it, s)
        if own:
            rown[g] = total.astype(BF16)
        else:
            sd[p] = total.astype(BF16)
            d_copy(p, z_of, g).start()

    def stage_y(it):
        for s in range(2):
            p = 2 * it + s
            first_all(p, s).wait()

            def over_x(y_of):
                total = part[p, owner_rows(x * NY + y_of), :].astype(F32)
                for n in range(NX - 1):
                    total = total + dr[p, owner_rows(2 * n + y_of), :].astype(F32)
                return total

            def over_y(x_of):
                return part[p, owner_rows(x_of * NY + yh), :].astype(F32) + dr[p, owner_rows(x_of), :].astype(F32)

            if s == 0:
                sc[p, 0:SLOTS, :] = over_x(1 - yh).astype(BF16)
            else:
                for n, (_, px) in enumerate(row):
                    sc[p, n * SLOTS:(n + 1) * SLOTS, :] = over_y(px).astype(BF16)
            second_copies(p, s)
            keep[p] = over_x(yh) if s == 0 else over_y(x)

    def stage_d(it, own):
        for s in range(2):
            p = 2 * it + s
            second_all(p, s).wait()
            total = keep[p]
            for n in range((6, 4)[s], 7):
                total = total + dr[p, n * SLOTS:(n + 1) * SLOTS, :].astype(F32)
            deliver(it, s, total, own)

    def stage_o(it, own):
        for s in range(2):
            p = 2 * it + s
            o_all(p).wait()
            total = part[p, owner_rows(owner), :].astype(F32)
            for n in range(OWN - 1):
                total = total + dr[p, n * SLOTS:(n + 1) * SLOTS, :].astype(F32)
            deliver(it, s, total, own)

    def step(it, carry):
        k = it - 1

        @pl.when(it == 1)
        def _():
            ring_begin(2)
            ring_begin(3)
            w_forward(2)

        @pl.when(it == 2)
        def _():
            w_forward(3)
            w_finish(2)
            project(2)

        @pl.when(it == 3)
        def _():
            w_finish(3)
            project(3)
            w_sent(2, (0, 1))
            w_sent(3, (0, 1))
            w_start(W_OUT)
            for n in range(5):
                back_copy(2, n).start()

        @pl.when(it == 10)
        def _():
            w_forward(W_OUT)

        @pl.when((it >= 1) & (it < STEPS - 1))
        def _():
            for side in range(2):
                z_of, g = piece(it, side)
                ring(side, k, z_of, g).wait_recv()

        @pl.when((it >= 1) & (k < 10))
        def _():
            z_of, g = piece(it, 0)
            ring(0, k + 4, z_of, g).start()

        @pl.when((it >= 1) & (k < 8))
        def _():
            z_of, g = piece(it, 1)
            ring(1, k + 4, z_of, g).start()

        @pl.when((k == 10) | (k == 11))
        def _():
            z_of, g = piece(it, 1)
            ring(1, k + 2, z_of, g).start()

        @pl.when((it >= LAG) & (it < CUT + LAG))
        def _():
            stage_y(it - LAG)

        @pl.when(it == LAG + LAG - 1)
        def _():
            stage_d(0, True)

        @pl.when((it > LAG + LAG - 1) & (it < CUT + LAG + LAG - 1))
        def _():
            stage_d(it - (LAG + LAG - 1), False)

        for side in range(2):
            z_of, g = piece(it, side)
            p = 2 * it + side
            attend(z_of, g, p)

        @pl.when(it < CUT)
        def _():
            for side in range(2):
                first_copies(2 * it + side, side)

        @pl.when(it >= CUT)
        def _():
            for side in range(2):
                for n in range(OWN - 1):
                    o_copy(2 * it + side, n).start()

        return carry

    lax.fori_loop(0, STEPS, step, 0)

    for it in range(STEPS - LAG, CUT):
        stage_y(it)
    for it in range(STEPS - (LAG + LAG - 1), CUT):
        stage_d(it, False)
    for it in range(CUT, STEPS - 1):
        stage_o(it, False)
    w_finish(W_OUT)
    for n in range(5):
        back_arrived(2, n)
    gates = silu(pg[0:SLOTS, :] + rg[0] + rg[1] + rg[2])
    stage_o(STEPS - 1, True)
    remote(rd, rd, x_send.at[0], d_recv, mirror).wait_recv()
    mixed = jnp.concatenate(
        [rown[g].astype(F32) + sum(rd[n, g].astype(F32) for n in range(NZ - 1)) for g in range(GROUPS)], axis=1
    )
    gated = (normed(mixed).astype(BF16).astype(F32) * gates).astype(BF16)
    projected = jnp.dot(gated, wo[...], preferred_element_type=F32)
    out_ref[...] = (cand_ref[...].astype(F32) + projected).astype(BF16)

    for n in range(len(pieces)):
        w_sent(n, (2, 3, 4, 5) if n < W_OUT else range(6))
    for n, (peer, _) in enumerate(flat):
        remote(st1.at[owner], st1.at[owner], st_send.at[0, n], st1_recv.at[owner], peer).wait_send()
    for n, (peer, _) in enumerate(column):
        remote(st2.at[z], st2.at[z], st_send.at[1, n], st2_recv.at[z], peer).wait_send()
    for n in range(5):
        in_copy(n).wait_send()
        back_copy(1, n).wait_send()
        back_copy(2, n).wait_send()
    for g in range(GROUPS):
        q_all(g).wait_send()

    def ring_sent(n, carry):
        for side in range(2):
            ring(side, n, z, 0).wait_send()
        return carry

    lax.fori_loop(0, 14, ring_sent, 0)

    def d_sent(n, carry):
        remote(sd.at[n], rd.at[0, 0], d_send.at[n], d_recv, mirror).wait_send()
        return carry

    lax.fori_loop(2, 2 * STEPS - 2, d_sent, 0)


def local(history, hist_len, cand_start, candidates, slot_cand, w_kv, w_qu, w_o):
    pieces = 2 * STEPS
    vmem = pl.BlockSpec(memory_space=pltpu.VMEM)
    smem = pl.BlockSpec(memory_space=pltpu.SMEM)
    anywhere = pl.BlockSpec(memory_space=pl.ANY)
    dma = pltpu.SemaphoreType.DMA
    out = pl.pallas_call(
        kernel,
        out_shape=jax.ShapeDtypeStruct((SLOTS, WIDTH), BF16),
        in_specs=[smem, smem, vmem, vmem, vmem, anywhere, anywhere, anywhere],
        out_specs=vmem,
        scratch_shapes=[
            pltpu.VMEM((QUARTER, 2 * WIDTH), BF16),
            pltpu.VMEM((WIDTH, 2 * WIDTH), BF16),
            pltpu.VMEM((WIDTH, WIDTH), BF16),
            pltpu.VMEM((SPAN, WIDTH), BF16),
            pltpu.VMEM((4, SLOTS, QUARTER), BF16),
            pltpu.VMEM((4 * SLOTS, QUARTER), BF16),
            pltpu.VMEM((4 * SLOTS, WIDTH), F32),
            pltpu.VMEM((4 * SLOTS, WIDTH), F32),
            pltpu.VMEM((3, SLOTS, WIDTH), F32),
            pltpu.VMEM((3, SLOTS, WIDTH), F32),
            pltpu.VMEM((GROUPS, BLOCKS, WIDE, HEADS * KBLK), BF16),
            pltpu.VMEM((GROUPS, BLOCKS, HEADS * KBLK, WIDE), BF16),
            pltpu.VMEM((NZ, GROUPS, ROWS, WIDE), BF16),
            pltpu.VMEM((NZ, BLOCKS, ROWS, 128), BF16),
            pltpu.VMEM((OWN, 8, 128), F32),
            pltpu.VMEM((NZ, 8, 128), F32),
            pltpu.VMEM((pieces, ROWS, WIDE), BF16),
            pltpu.VMEM((pieces, (OWN - 1) * SLOTS, WIDE), BF16),
            pltpu.VMEM((pieces, (NX - 1) * SLOTS, WIDE), BF16),
            pltpu.VMEM((pieces, SLOTS, WIDE), F32),
            pltpu.VMEM((pieces, SLOTS, WIDE), BF16),
            pltpu.VMEM((NZ - 1, GROUPS, SLOTS, WIDE), BF16),
            pltpu.VMEM((GROUPS, SLOTS, WIDE), BF16),
            dma((1 + GROUPS, 6)), dma((1 + GROUPS, 6)), dma((1 + GROUPS, 2)),
            dma((3, 5)), dma((3, 5)), dma,
            dma((2, 7)), dma((OWN,)), dma((NZ,)),
            dma((GROUPS,)), dma((GROUPS,)),
            dma((2, 14)), dma((2, 14)),
            dma((pieces,)), dma((pieces,)),
            dma((pieces,)), dma((pieces,)),
            dma((pieces,)), dma,
        ],
        compiler_params=pltpu.CompilerParams(
            collective_id=0, has_side_effects=True, vmem_limit_bytes=60 * 2**20
        ),
    )(hist_len, cand_start, slot_cand, history[0], candidates[0], w_kv, w_qu, w_o)
    return out[None]


def solution(mesh):
    in_specs = (
        P("user", "seq", None),
        P("user"),
        P("user", None),
        P("user", "seq", None),
        P("user", "seq"),
        P("user", None),
        P("user", None),
        P("user", None),
    )
    out_specs = P("user", "seq", None)
    return jax.shard_map(local, mesh=mesh, in_specs=in_specs, out_specs=out_specs, check_vma=False)
```

time: 122 us -> 98.8 us (0.81)
  Pallas kernels: 120 us -> 96 us
    pallas_call x1, Pallas kernels: 120 us -> 96 us  [local(): pl.pallas_call(kernel, out_shape=jax.ShapeDtypeStruct((SLOTS, WIDTH), BF1...]
where the time goes in v2:
time: 98.8 us; the launch traced here: 98.1 us
  Pallas kernels  96 us (97%)
  local copies, waits for them, and re-layouts  1.47 us (1%)
    pallas_call x1, Pallas kernels, local(): pl.pallas_call(kernel, out_shape=jax.ShapeDtypeStruct((SLOTS, WIDTH), BF1...  96 us

profile of v2, /device:TPU:8, one launch (start us, length us, event | category | flops | bytes accessed | tf_op | source)
XLA Modules:
  0.0 98.1 jit_solution(3065408911057294130)
XLA Ops:
  0.7 96.0 %shard_map.82 = bf16[32,1024]{1,0:T(8,128)(2,1)} custom-call(s32[1]{0:T(128)S(6)} %copy.10.len_ref, s32[1,16]{1,0:T(1,128)} %start_ref.1, s32[1,32]{1,0:T(1,128)} %slot_ref.1, bf16[512,1024]{1,0:T(8,128)(2,1)} %bitcast.3, bf16[32,1024]{1,0:T(8,128)(2,1)} %bitcast.5, bf16[256,2048]{1,0:T(8,128)(2,1)} %wkv_hbm.1, bf16[256,2048]{1,0:T(8,128)(2,1)} %wqu_hbm.1, ...), custom_call_target="tpu_custom_call" | custom-call | tf_op jit(solution)/shard_map/pallas_call | solution.py:565
  96.6 1.5 %copy.11 = bf16[1,32,1024]{2,1,0:T(8,128)(2,1)} copy(bf16[1,32,1024]{2,1,0:T(8,128)(2,1)} %bitcast.4) | data formatting | bytes 131072

commit v3 on v2

--- a/solution.py
+++ b/solution.py
@@ -307,9 +307,9 @@
 
     lax.fori_loop(0, NZ, make_masks, 0)
 
+    ring_begin(0)
     w_finish(1)
     project(1)
-    ring_begin(0)
     ring_begin(1)
 
     def piece(it, side):
@@ -434,11 +434,11 @@
         @pl.when(it == 1)
         def _():
             ring_begin(2)
+            w_forward(2)
+
+        @pl.when(it == 2)
+        def _():
             ring_begin(3)
-            w_forward(2)
-
-        @pl.when(it == 2)
-        def _():
             w_forward(3)
             w_finish(2)
             project(2)
@@ -450,6 +450,9 @@
             w_sent(2, (0, 1))
             w_sent(3, (0, 1))
             w_start(W_OUT)
+
+        @pl.when(it == 9)
+        def _():
             for n in range(5):
                 back_copy(2, n).start()
 
@@ -463,15 +466,28 @@
                 z_of, g = piece(it, side)
                 ring(side, k, z_of, g).wait_recv()
 
-        @pl.when((it >= 1) & (k < 10))
-        def _():
-            z_of, g = piece(it, 0)
-            ring(0, k + 4, z_of, g).start()
-
-        @pl.when((it >= 1) & (k < 8))
-        def _():
-            z_of, g = piece(it, 1)
-            ring(1, k + 4, z_of, g).start()
+        def pass_on(side, item):
+            z_of, g = piece(item + 1, side)
+            ring(side, item + 4, z_of, g).start()
+
+        @pl.when(it == 2)
+        def _():
+            pass_on(0, 0)
+            pass_on(1, 0)
+
+        @pl.when(it == 3)
+        def _():
+            for item in (1, 2):
+                pass_on(0, item)
+                pass_on(1, item)
+
+        @pl.when((it >= 4) & (k < 10))
+        def _():
+            pass_on(0, k)
+
+        @pl.when((it >= 4) & (k < 8))
+        def _():
+            pass_on(1, k)
 
         @pl.when((k == 10) | (k == 11))
         def _():
@@ -489,6 +505,10 @@
         @pl.when((it > LAG + LAG - 1) & (it < CUT + LAG + LAG - 1))
         def _():
             stage_d(it - (LAG + LAG - 1), False)
+
+        @pl.when(it == STEPS - 1)
+        def _():
+            stage_o(CUT, False)
 
         for side in range(2):
             z_of, g = piece(it, side)
@@ -514,7 +534,7 @@
         stage_y(it)
     for it in range(STEPS - (LAG + LAG - 1), CUT):
         stage_d(it, False)
-    for it in range(CUT, STEPS - 1):
+    for it in range(CUT + 1, STEPS - 1):
         stage_o(it, False)
     w_finish(W_OUT)
     for n in range(5):

time: 98.8 us -> 96.4 us (0.976)
  Pallas kernels: 96 us -> 94.1 us
    pallas_call x1, Pallas kernels: 96 us -> 94.1 us  [local(): pl.pallas_call(kernel, out_shape=jax.ShapeDtypeStruct((SLOTS, WIDTH), BF1...]
where the time goes in v3:
time: 96.4 us; the launch traced here: 96.2 us
  Pallas kernels  94.1 us (98%)
  local copies, waits for them, and re-layouts  1.47 us (2%)
    pallas_call x1, Pallas kernels, local(): pl.pallas_call(kernel, out_shape=jax.ShapeDtypeStruct((SLOTS, WIDTH), BF1...  94.1 us

profile of v3, /device:TPU:8, one launch (start us, length us, event | category | flops | bytes accessed | tf_op | source)
XLA Modules:
  0.0 96.2 jit_solution(14115663051683310840)
XLA Ops:
  0.7 94.1 %shard_map.82 = bf16[32,1024]{1,0:T(8,128)(2,1)} custom-call(s32[1]{0:T(128)S(6)} %copy.10.len_ref, s32[1,16]{1,0:T(1,128)} %start_ref.1, s32[1,32]{1,0:T(1,128)} %slot_ref.1, bf16[512,1024]{1,0:T(8,128)(2,1)} %bitcast.3, bf16[32,1024]{1,0:T(8,128)(2,1)} %bitcast.5, bf16[256,2048]{1,0:T(8,128)(2,1)} %wkv_hbm.1, bf16[256,2048]{1,0:T(8,128)(2,1)} %wqu_hbm.1, ...), custom_call_target="tpu_custom_call" | custom-call | tf_op jit(solution)/shard_map/pallas_call | solution.py:585
  94.8 1.5 %copy.11 = bf16[1,32,1024]{2,1,0:T(8,128)(2,1)} copy(bf16[1,32,1024]{2,1,0:T(8,128)(2,1)} %bitcast.4) | data formatting | bytes 131072

commit v4 on v3

--- a/solution.py
+++ b/solution.py
@@ -209,7 +209,7 @@
     pltpu.make_async_copy(wqu_hbm, wqu, p_local).wait()
     for n in range(5):
         in_arrived(n)
-    pq[...] = jnp.dot(cin[...], wqu[:, :WIDTH], preferred_element_type=F32)
+    pq[...] = jnp.dot(cin[...], wqu[:, :WIDTH], preferred_element_type=F32).astype(BF16)
     for n in range(5):
         back_copy(1, n).start()
 
@@ -231,7 +231,7 @@
 
     for n in range(5):
         back_arrived(1, n)
-    queries = silu(pq[0:SLOTS, :] + rq[0] + rq[1] + rq[2]).astype(BF16)
+    queries = silu(pq[0:SLOTS, :].astype(F32) + sum(rq[n].astype(F32) for n in range(3))).astype(BF16)
     mine = pl.ds(pl.multiple_of(owner * SLOTS, SLOTS), SLOTS)
 
     def q_copy(g, n):
@@ -286,7 +286,7 @@
     for g in range(2, GROUPS):
         for n in range(OWN - 1):
             q_copy(g, n).start()
-    pg[...] = jnp.dot(cin[...], wqu[:, WIDTH:], preferred_element_type=F32)
+    pg[...] = jnp.dot(cin[...], wqu[:, WIDTH:], preferred_element_type=F32).astype(BF16)
     w_finish(0)
     project(0)
     for n, (peer, pz) in enumerate(column):
@@ -539,7 +539,7 @@
     w_finish(W_OUT)
     for n in range(5):
         back_arrived(2, n)
-    gates = silu(pg[0:SLOTS, :] + rg[0] + rg[1] + rg[2])
+    gates = silu(pg[0:SLOTS, :].astype(F32) + sum(rg[n].astype(F32) for n in range(3)))
     stage_o(STEPS - 1, True)
     remote(rd, rd, x_send.at[0], d_recv, mirror).wait_recv()
     mixed = jnp.concatenate(
@@ -594,10 +594,10 @@
             pltpu.VMEM((SPAN, WIDTH), BF16),
             pltpu.VMEM((4, SLOTS, QUARTER), BF16),
             pltpu.VMEM((4 * SLOTS, QUARTER), BF16),
-            pltpu.VMEM((4 * SLOTS, WIDTH), F32),
-            pltpu.VMEM((4 * SLOTS, WIDTH), F32),
-            pltpu.VMEM((3, SLOTS, WIDTH), F32),
-            pltpu.VMEM((3, SLOTS, WIDTH), F32),
+            pltpu.VMEM((4 * SLOTS, WIDTH), BF16),
+            pltpu.VMEM((4 * SLOTS, WIDTH), BF16),
+            pltpu.VMEM((3, SLOTS, WIDTH), BF16),
+            pltpu.VMEM((3, SLOTS, WIDTH), BF16),
             pltpu.VMEM((GROUPS, BLOCKS, WIDE, HEADS * KBLK), BF16),
             pltpu.VMEM((GROUPS, BLOCKS, HEADS * KBLK, WIDE), BF16),
             pltpu.VMEM((NZ, GROUPS, ROWS, WIDE), BF16),

time: 96.4 us -> 99.6 us (1.033)
  Pallas kernels: 94.1 us -> 97.3 us
    pallas_call x1, Pallas kernels: 94.1 us -> 97.3 us  [local(): pl.pallas_call(kernel, out_shape=jax.ShapeDtypeStruct((SLOTS, WIDTH), BF1...]
where the time goes in v4:
time: 99.6 us; the launch traced here: 99.5 us
  Pallas kernels  97.3 us (98%)
  local copies, waits for them, and re-layouts  1.47 us (1%)
    pallas_call x1, Pallas kernels, local(): pl.pallas_call(kernel, out_shape=jax.ShapeDtypeStruct((SLOTS, WIDTH), BF1...  97.3 us

profile of v4, /device:TPU:8, one launch (start us, length us, event | category | flops | bytes accessed | tf_op | source)
XLA Modules:
  0.0 99.5 jit_solution(12823954162973924315)
XLA Ops:
  0.7 97.3 %shard_map.82 = bf16[32,1024]{1,0:T(8,128)(2,1)} custom-call(s32[1]{0:T(128)S(6)} %copy.10.len_ref, s32[1,16]{1,0:T(1,128)} %start_ref.1, s32[1,32]{1,0:T(1,128)} %slot_ref.1, bf16[512,1024]{1,0:T(8,128)(2,1)} %bitcast.3, bf16[32,1024]{1,0:T(8,128)(2,1)} %bitcast.5, bf16[256,2048]{1,0:T(8,128)(2,1)} %wkv_hbm.1, bf16[256,2048]{1,0:T(8,128)(2,1)} %wqu_hbm.1, ...), custom_call_target="tpu_custom_call" | custom-call | tf_op jit(solution)/shard_map/pallas_call | solution.py:585
  98.0 1.5 %copy.11 = bf16[1,32,1024]{2,1,0:T(8,128)(2,1)} copy(bf16[1,32,1024]{2,1,0:T(8,128)(2,1)} %bitcast.4) | data formatting | bytes 131072
